TPU v7x, 256 devices: a whole 4x4x8 slice. The times are simulated.
256 devices in a mesh: dp: 16 (over x_lo, z), expert: 16 (over y, x_hi, core).
Axes of the slice: x: 4 (x_hi: 2, x_lo: 2; x = x_hi * 2 + x_lo), y: 4, z: 8, core: 2. Of those that a mesh axis runs over, the one named last changes fastest.
Arguments:
- images: bfloat16 [512, 256, 768], P(('dp', 'expert')), may hold values from -64 to 64
- out_grad: bfloat16 [512, 256, 768], P(('dp', 'expert')), may hold values from -6 to 6
- router: bfloat16 [768, 128], replicated, may hold values from -0.14505926 to 0.14505926
- w_in: bfloat16 [16, 768, 3072], P('expert'), may hold values from -0.21875 to 0.21875
- w_out: bfloat16 [16, 3072, 768], P('expert'), may hold values from -0.109375 to 0.109375
Outputs:
- image_grad: bfloat16 [512, 256, 768], P(('dp', 'expert'))
- router_grad: float32 [768, 128], replicated
- w_in_grad: bfloat16 [16, 768, 3072], P('expert', 'dp')
- w_out_grad: bfloat16 [16, 3072, 768], P('expert', 'dp')
All inputs are finite; a program needn't handle non-finite values.
Results may differ from a plain program's by a relative error of at most 0.023.
Values may be sent and summed in bfloat16 or wider, within the bound.
A program may use at most 64 MiB of HBM per device.

v0:
```python
import jax
import jax.numpy as jnp
from jax import lax
from jax.sharding import PartitionSpec as P


def contract_first(left, right):
    return lax.dot_general(
        left, right, (((0,), (0,)), ((), ())), preferred_element_type=jnp.float32
    )


def contract_last(left, right):
    return lax.dot_general(
        left, right, (((1,), (1,)), ((), ())), preferred_element_type=jnp.float32
    )


def local(images, out_grad, router, w_in, w_out):
    weight_in = w_in[0]
    weight_out = w_out[0]
    width = images.shape[2]
    logits = jnp.einsum("bmd,ds->bms", images, router, preferred_element_type=jnp.float32)
    dispatch = jax.nn.softmax(logits, axis=1)
    combine = jax.nn.softmax(logits, axis=2)
    disp_bf = dispatch.astype(jnp.bfloat16)
    comb_bf = combine.astype(jnp.bfloat16)
    slot_in = jnp.einsum(
        "bms,bmd->bsd", disp_bf, images, preferred_element_type=jnp.float32
    ).astype(jnp.bfloat16)
    slot_grad = jnp.einsum(
        "bms,bmd->bsd", comb_bf, out_grad, preferred_element_type=jnp.float32
    ).astype(jnp.bfloat16)
    arrived = lax.all_to_all(slot_in, "expert", split_axis=1, concat_axis=0, tiled=True)
    held_shape = arrived.shape
    expert_rows = arrived.reshape(-1, width)
    pre_act = jnp.dot(expert_rows, weight_in, preferred_element_type=jnp.float32)
    hidden_act, backward = jax.vjp(jax.nn.gelu, pre_act)
    hidden_bf = hidden_act.astype(jnp.bfloat16)
    slot_out = jnp.dot(hidden_bf, weight_out, preferred_element_type=jnp.float32).astype(
        jnp.bfloat16
    )
    out_home = lax.all_to_all(
        slot_out.reshape(held_shape), "expert", split_axis=0, concat_axis=1, tiled=True
    )
    grad_rows = lax.all_to_all(
        slot_grad, "expert", split_axis=1, concat_axis=0, tiled=True
    ).reshape(-1, width)
    delta_hidden = contract_last(grad_rows, weight_out)
    delta_act = backward(delta_hidden)[0].astype(jnp.bfloat16)
    slot_dx = contract_last(delta_act, weight_in).astype(jnp.bfloat16)
    dx_home = lax.all_to_all(
        slot_dx.reshape(held_shape), "expert", split_axis=0, concat_axis=1, tiled=True
    )
    grad_first = contract_first(expert_rows, delta_act)
    grad_second = contract_first(hidden_bf, grad_rows)
    up_share, down_share = (
        lax.psum_scatter(
            grad_first.astype(jnp.bfloat16), "dp", scatter_dimension=0, tiled=True
        ).astype(jnp.float32),
        lax.psum_scatter(
            grad_second.astype(jnp.bfloat16), "dp", scatter_dimension=0, tiled=True
        ).astype(jnp.float32),
    )
    dcomb = jnp.einsum("bmd,bsd->bms", out_grad, out_home, preferred_element_type=jnp.float32)
    ddisp = jnp.einsum("bmd,bsd->bms", images, dx_home, preferred_element_type=jnp.float32)
    dlogits = combine * (dcomb - jnp.sum(combine * dcomb, axis=2, keepdims=True))
    dlogits = dlogits + dispatch * (ddisp - jnp.sum(dispatch * ddisp, axis=1, keepdims=True))
    dlogits = dlogits.astype(jnp.bfloat16)
    image_grad = jnp.einsum("bms,bsd->bmd", disp_bf, dx_home, preferred_element_type=jnp.float32)
    image_grad = image_grad + jnp.einsum(
        "bms,ds->bmd", dlogits, router, preferred_element_type=jnp.float32
    )
    router_part = jnp.einsum("bmd,bms->ds", images, dlogits, preferred_element_type=jnp.float32)
    router_grad = lax.psum(router_part, ("dp", "expert"))
    return (
        image_grad.astype(jnp.bfloat16),
        router_grad,
        up_share.astype(jnp.bfloat16)[None],
        down_share.astype(jnp.bfloat16)[None],
    )


def solution(mesh):
    return jax.shard_map(
        local,
        mesh=mesh,
        in_specs=(
            P(("dp", "expert"), None, None),
            P(("dp", "expert"), None, None),
            P(),
            P("expert", None, None),
            P("expert", None, None),
        ),
        out_specs=(
            P(("dp", "expert"), None, None),
            P(),
            P("expert", "dp", None),
            P("expert", "dp", None),
        ),
        check_vma=False,
    )
```

profile of v0, /device:TPU:1, one launch (start us, length us, event | category | flops | bytes accessed | tf_op | source)
XLA Modules:
  0.0 367.7 jit_solution(13586594647816461843)
XLA Ops:
  8.0 0.0 copy-start
  8.0 1.1 copy-done
  9.1 1.3 fusion.56
  10.4 0.9 fusion.64
  11.3 2.2 convolution_convert_fusion.3
  13.5 1.2 copy.38
  14.7 8.4 %all-to-all-start = ((bf16[2,128,768]{2,0,1:T(2,128)(2,1)}), bf16[2,128,768]{2,0,1:T(2,128)(2,1)S(1)}, u32[]{:S(2)}, u32[]{:S(2)}) async-start(bf16[2,128,768]{2,0,1:T(2,128)(2,1)} %copy.38), calls=%async_computation | async-start | bytes 786432 | tf_op jit(solution)/shard_map/all_to_all | solution.py:46
  23.1 0.8 fusion.63
  23.9 0.4 convolution_convert_fusion.2
  24.3 1.2 copy.42
  25.4 7.6 %all-to-all-done = bf16[2,128,768]{2,0,1:T(2,128)(2,1)S(1)} async-done(((bf16[2,128,768]{2,0,1:T(2,128)(2,1)}), bf16[2,128,768]{2,0,1:T(2,128)(2,1)S(1)}, u32[]{:S(2)}, u32[]{:S(2)}) %all-to-all-start) | async-done | bytes 393248 | tf_op jit(solution)/shard_map/all_to_all | solution.py:46
  33.0 4.5 %all-to-all-start.1 = ((bf16[2,128,768]{2,0,1:T(2,128)(2,1)}), bf16[2,128,768]{2,0,1:T(2,128)(2,1)S(1)}, u32[]{:S(2)}, u32[]{:S(2)}) async-start(bf16[2,128,768]{2,0,1:T(2,128)(2,1)} %copy.42), calls=%async_computation.1 | async-start | bytes 786432 | tf_op jit(solution)/shard_map/all_to_all | solution.py:34
  37.6 0.8 copy.40
  38.3 9.2 %all-to-all-done.1 = bf16[2,128,768]{2,0,1:T(2,128)(2,1)S(1)} async-done(((bf16[2,128,768]{2,0,1:T(2,128)(2,1)}), bf16[2,128,768]{2,0,1:T(2,128)(2,1)S(1)}, u32[]{:S(2)}, u32[]{:S(2)}) %all-to-all-start.1) | async-done | bytes 393248 | tf_op jit(solution)/shard_map/all_to_all | solution.py:34
  47.5 0.0 slice-start
  47.6 0.0 slice-start.1
  47.6 3.9 %fusion.6 = f32[256,3072]{1,0:T(8,128)S(1)} fusion(bf16[256,768]{1,0:T(8,128)(2,1)S(1)} %bitcast.84, bf16[1,768,3072]{2,1,0:T(8,128)(2,1)} %param.8), kind=kOutput, calls=%fused_computation.8 | convolution fusion | flops 1207959552 | bytes 8257536 | tf_op jit(solution)/shard_map/dot_general | solution.py:37
  51.5 0.0 copy-start.3
  51.5 1.7 copy-done.3
  53.1 0.0 slice-done
  53.1 0.0 slice-done.1
  53.1 2.7 fusion.32
  55.8 4.5 %all-to-all-start.3 = ((bf16[32,8,768]{2,1,0:T(8,128)(2,1)}), bf16[32,8,768]{2,1,0:T(8,128)(2,1)S(1)}, u32[]{:S(2)}, u32[]{:S(2)}) async-start(bf16[32,8,768]{2,1,0:T(8,128)(2,1)} %fusion.32), calls=%async_computation.3 | async-start | bytes 786432 | tf_op jit(solution)/shard_map/all_to_all | solution.py:43
  60.4 6.1 %fusion.18 = bf16[256,3072]{1,0:T(8,128)(2,1)S(1)} fusion(f32[256,3072]{1,0:T(8,128)} %copy-done.3, bf16[256,768]{1,0:T(8,128)(2,1)} %bitcast.89, bf16[1,3072,768]{2,1,0:T(8,128)(2,1)} %param.9), kind=kOutput, calls=%fused_computation.22 | convolution fusion | flops 1223688192 | bytes 9830400 | tf_op jit(solution)/shard_map/dot_general | solution.py:14
  66.4 4.5 %fusion.29 = bf16[32,8,768]{2,1,0:T(8,128)(2,1)} fusion(bf16[256,3072]{1,0:T(8,128)(2,1)S(1)} %fusion.18, bf16[1,768,3072]{2,1,0:T(8,128)(2,1)} %param.8), kind=kOutput, calls=%fused_computation.31 | convolution fusion | flops 1208156160 | bytes 6684672 | tf_op jit(solution)/shard_map/dot_general | solution.py:14
  70.9 0.0 all-to-all-done.3
  71.0 0.0 copy-start.1
  71.0 0.7 copy-done.1
  71.7 7.3 %all-to-all-start.2 = ((bf16[32,8,768]{2,1,0:T(8,128)(2,1)}), bf16[32,8,768]{2,1,0:T(8,128)(2,1)S(1)}, u32[]{:S(2)}, u32[]{:S(2)}) async-start(bf16[32,8,768]{2,1,0:T(8,128)(2,1)} %fusion.29), calls=%async_computation.2 | async-start | bytes 786432 | tf_op jit(solution)/shard_map/all_to_all | solution.py:52
  79.0 0.0 all-reduce.2.cloned.1.call-start
  79.0 2.3 convolution_bitcast_fusion.2
  81.3 7.5 %all-to-all-done.2 = bf16[32,8,768]{2,1,0:T(8,128)(2,1)S(1)} async-done(((bf16[32,8,768]{2,1,0:T(8,128)(2,1)}), bf16[32,8,768]{2,1,0:T(8,128)(2,1)S(1)}, u32[]{:S(2)}, u32[]{:S(2)}) %all-to-all-start.2) | async-done | bytes 393248 | tf_op jit(solution)/shard_map/all_to_all | solution.py:52
  88.9 0.4 convolution_bitcast_fusion.1
  89.2 1.8 fusion.39
  91.1 4.6 %convolution_bitcast_fusion = f32[768,128]{0,1:T(8,128)} fusion(bf16[2,256,768]{2,1,0:T(8,128)(2,1)S(1)} %copy-done, f32[2,256,128]{2,1,0:T(8,128)} %fusion.39, f32[2,256,128]{2,1,0:T(8,128)} %convolution_bitcast_fusion.2, f32[2,256,128]{2,1,0:T(8,128)} %get-tuple-element.23, f32[2,256]{1,0:T(2,128)S(1)} %get-tuple-element.22), kind=kOutput, calls=%fused_computation.33 | convolution fusion | flops 101122688 | bytes 1968128 | tf_op jit(solution)/shard_map/bmd,bms->ds/dot_general | solution.py:74
  95.7 0.0 all-reduce.2.cloned.1.call-update
  95.7 0.2 reduce-scatter.5.cloned.1.call-start
  95.9 6.3 %convolution_convert_fusion = bf16[3072,768]{1,0:T(8,128)(2,1)} fusion(bf16[256,768]{1,0:T(8,128)(2,1)} %bitcast.90, f32[256,3072]{1,0:T(8,128)} %copy-done.3), kind=kOutput, calls=%fused_computation.4 | convolution fusion | flops 1217396736 | bytes 8257536 | tf_op jit(solution)/shard_map/dot_general | solution.py:8
  102.2 0.0 reduce-scatter.5.cloned.1.call-update
  102.3 0.0 reduce-scatter.3.cloned.1.call-start
  102.3 3.6 convolution_convert_fusion.1
  105.9 0.0 copy-start.2
  105.9 0.0 reduce-scatter.3.cloned.1.call-update
  105.9 0.4 fusion.49
  106.3 0.5 copy-done.2
  106.8 4.4 %add_convert_fusion = bf16[2,256,768]{2,1,0:T(8,128)(2,1)} fusion(f32[2,256,768]{2,1,0:T(8,128)S(1)} %fusion.49, f32[2,256,128]{2,1,0:T(8,128)} %fusion.39, f32[2,256,128]{2,1,0:T(8,128)} %convolution_bitcast_fusion.2, bf16[768,128]{1,0:T(8,128)(2,1)S(1)} %copy-done.2, f32[2,256,128]{2,1,0:T(8,128)} %get-tuple-element.23, f32[2,256]{1,0:T(2,128)S(1)} %get-tuple-element.22), kind=kOutput, calls=%fused_computation.24 | convolution fusion | flops 101909120 | bytes 3344384 | tf_op jit(solution)/shard_map/bms,ds->bmd/dot_general | solution.py:71
  111.3 247.1 %all-reduce.2.cloned.1.call-done = f32[768,128]{0,1:T(8,128)} async-done(((f32[768,128]{0,1:T(8,128)}), f32[768,128]{0,1:T(8,128)}) %all-reduce.2.cloned.1.call-update) | async-done | bytes 393232 | tf_op jit(solution)/shard_map/psum | solution.py:75
  358.4 1.9 copy.50
  360.3 0.0 reduce-scatter.5.cloned.1.call-done
  360.3 0.0 reduce-scatter.3.cloned.1.call-done
  (4 shorter events, 0.1 us)
Async XLA Ops:
  8.0 1.1 copy-start
  14.7 18.3 %all-to-all-start = ((bf16[2,128,768]{2,0,1:T(2,128)(2,1)}), bf16[2,128,768]{2,0,1:T(2,128)(2,1)S(1)}, u32[]{:S(2)}, u32[]{:S(2)}) async-start(bf16[2,128,768]{2,0,1:T(2,128)(2,1)} %copy.38), calls=%async_computation | async-start | bytes 786432 | tf_op jit(solution)/shard_map/all_to_all | solution.py:46
  33.0 14.5 %all-to-all-start.1 = ((bf16[2,128,768]{2,0,1:T(2,128)(2,1)}), bf16[2,128,768]{2,0,1:T(2,128)(2,1)S(1)}, u32[]{:S(2)}, u32[]{:S(2)}) async-start(bf16[2,128,768]{2,0,1:T(2,128)(2,1)} %copy.42), calls=%async_computation.1 | async-start | bytes 786432 | tf_op jit(solution)/shard_map/all_to_all | solution.py:34
  47.5 5.6 %slice-start = ((s8[4718592]{0:T(1024)(128)(4,1)}), s8[4194304]{0:T(1024)(128)(4,1)S(1)}, s32[]{:S(2)}) async-start(s8[4718592]{0:T(1024)(128)(4,1)} %bitcast.91), calls=%async_computation.9 | async-start | bytes 8388608
  47.6 5.6 %slice-start.1 = ((s8[4718592]{0:T(1024)(128)(4,1)}), s8[524288]{0:T(1024)(128)(4,1)S(1)}, s32[]{:S(2)}) async-start(s8[4718592]{0:T(1024)(128)(4,1)} %bitcast.91), calls=%async_computation.10 | async-start | bytes 1048576
  51.5 1.7 copy-start.3
  55.8 15.1 %all-to-all-start.3 = ((bf16[32,8,768]{2,1,0:T(8,128)(2,1)}), bf16[32,8,768]{2,1,0:T(8,128)(2,1)S(1)}, u32[]{:S(2)}, u32[]{:S(2)}) async-start(bf16[32,8,768]{2,1,0:T(8,128)(2,1)} %fusion.32), calls=%async_computation.3 | async-start | bytes 786432 | tf_op jit(solution)/shard_map/all_to_all | solution.py:43
  71.0 0.7 copy-start.1
  71.7 17.2 %all-to-all-start.2 = ((bf16[32,8,768]{2,1,0:T(8,128)(2,1)}), bf16[32,8,768]{2,1,0:T(8,128)(2,1)S(1)}, u32[]{:S(2)}, u32[]{:S(2)}) async-start(bf16[32,8,768]{2,1,0:T(8,128)(2,1)} %fusion.29), calls=%async_computation.2 | async-start | bytes 786432 | tf_op jit(solution)/shard_map/all_to_all | solution.py:52
  79.0 279.4 %all-reduce.2.cloned.1.call-start = ((), (), s32[]{:S(2)}) async-start(), calls=%async_computation.6 | async-start | bytes 786432 | tf_op jit(solution)/shard_map/psum | solution.py:75
  95.7 264.6 %reduce-scatter.5.cloned.1.call-start = ((), (), s32[]{:S(2)}) async-start(), calls=%async_computation.8 | async-start | bytes 5013504 | tf_op jit(solution)/shard_map/reduce_scatter | solution.py:61
  102.3 258.0 %reduce-scatter.3.cloned.1.call-start = ((), (), s32[]{:S(2)}) async-start(), calls=%async_computation.7 | async-start | bytes 5013504 | tf_op jit(solution)/shard_map/reduce_scatter | solution.py:58
  105.9 0.9 copy-start.2
Sparse Core Ops, SparseCore 0:
  95.8 262.5 all-reduce.1
Sparse Core Ops, SparseCore 1:
  102.4 70.1 reduce-scatter.4
  175.5 78.2 reduce-scatter.2
where the time goes:
time: 369 us; the launch traced here: 368 us
  waiting for transfers between devices  271 us (73%)
  matrix products  43 us (12%)
  starting transfers between devices  25 us (7%)
  between operations  15.6 us (4%)
  local copies, waits for them, and re-layouts  9.14 us (2%)
    psum x1, waiting for transfers between devices, local(): router_grad = lax.psum(router_part, ('dp', 'expert'))  247 us
    dot_general x2, matrix products, contract_last(): lax.dot_general(left, right, (((1,), (1,)), ((), ())), preferred_element_...  10.6 us
    dot_general x2, matrix products, contract_first(): lax.dot_general(left, right, (((0,), (0,)), ((), ())), preferred_element_...  9.91 us
    all_to_all x1, waiting for transfers between devices, local(): lax.all_to_all(slot_in, 'expert', split_axis=1, concat_axis=0, tiled=True)  9.16 us
    all_to_all x1, starting transfers between devices, local(): lax.all_to_all(slot_grad, 'expert', split_axis=1, concat_axis=0, tiled=True)  8.45 us
    all_to_all x1, waiting for transfers between devices, local(): lax.all_to_all(slot_grad, 'expert', split_axis=1, concat_axis=0, tiled=True)  7.59 us
    all_to_all x1, waiting for transfers between devices, local(): lax.all_to_all(slot_dx.reshape(held_shape), 'expert', split_axis=0, conca...  7.54 us
  transfers between devices with their start and end apart: 7, of which 4 were waited for; matrix products, arithmetic and copies ran while one was open for 9% of the time, Pallas kernels for 0%

commit v1 on v0

v1 whole, which is shorter than its diff:
```python
import math

import jax
import jax.numpy as jnp
from jax import lax
from jax.experimental import pallas as pl
from jax.experimental.pallas import tpu as pltpu
from jax.sharding import PartitionSpec as P

MESH = pl.DeviceIdType.MESH
BF = jnp.bfloat16
F32 = jnp.float32

D = 768
H = 3072
M = 256
S = 128
E = 16
NZ = 8
PER = 2
SPE = 8
BLK = PER * SPE
ROWS = E * BLK
TILE = 512
NT = H // TILE
HALF_T = NT // 2
CH_IN = D // (2 * NZ)
CH_OUT = H // (2 * NZ)
C0 = math.sqrt(2.0 / math.pi)
C1 = 0.044715


def dot(a, b, ca, cb):
    return lax.dot_general(a, b, (((ca,), (cb,)), ((), ())), preferred_element_type=F32)


def kernel(
    images, out_grad, router, w_in_hbm, w_out_hbm,
    image_grad, router_grad_t, w_in_share, w_out_share,
    w_in, w_out, disp, comb, sb_in, sb_grad, x_rows, g_rows,
    hid, gp, da, xt, gw_out, gw_in,
    ro_half, ro_full, ri_half, ri_full,
    so_send, dx_send, so_home, dx_home,
    rpart, r_a, r_b1, b_mine, r_b2, c_mine, r_c,
    w_sem, a2a_send, a2a_recv, rs_send, rs_recv, ar_send, ar_recv, loc_sem,
):
    d = lax.axis_index("dp")
    e = lax.axis_index("expert")
    pair = d // NZ
    z = d % NZ
    other_dp = (1 - pair) * NZ + z

    def zdev(k):
        return (pair * NZ + (z + k) % NZ, e)

    def w_copy(k):
        t = (HALF_T * pair + k) % NT
        return (
            pltpu.make_async_copy(w_in_hbm.at[:, pl.ds(pl.multiple_of(t * TILE, TILE), TILE)], w_in.at[k], w_sem.at[0, k]),
            pltpu.make_async_copy(w_out_hbm.at[pl.ds(pl.multiple_of(t * TILE, TILE), TILE), :], w_out.at[k], w_sem.at[1, k]),
        )

    for k in range(NT):
        for c in w_copy(k):
            c.start()

    barrier = pltpu.get_barrier_semaphore()

    def greet(k, _):
        to = (e + k) % E
        pl.semaphore_signal(barrier, inc=1, device_id=(other_dp, to), device_id_type=MESH)
        return 0

    lax.fori_loop(0, E, greet, 0)

    def greet_own(k, _):
        pl.semaphore_signal(barrier, inc=1, device_id=(d, (e + k) % E), device_id_type=MESH)
        return 0

    lax.fori_loop(1, E, greet_own, 0)
    for k in range(1, NZ):
        pl.semaphore_signal(barrier, inc=1, device_id=zdev(k), device_id_type=MESH)

    def spread(src, dst, n):
        pltpu.make_async_copy(src.at[e], dst.at[0, e], a2a_recv.at[n]).start()

        def far(k, _):
            to = (e + k) % E
            pltpu.make_async_remote_copy(
                src_ref=src.at[to], dst_ref=dst.at[1, e],
                send_sem=a2a_send.at[n, 1], recv_sem=a2a_recv.at[n],
                device_id=(other_dp, to), device_id_type=MESH,
            ).start()
            return 0

        def near(k, _):
            to = (e + k) % E
            pltpu.make_async_remote_copy(
                src_ref=src.at[to], dst_ref=dst.at[0, e],
                send_sem=a2a_send.at[n, 0], recv_sem=a2a_recv.at[n],
                device_id=(d, to), device_id_type=MESH,
            ).start()
            return far(k, 0)

        far(0, 0)
        lax.fori_loop(1, E, near, 0)

    def wait_bytes(ref, sem):
        pltpu.make_async_copy(ref, ref, sem).wait()

    def back(src, dst, n):
        pltpu.make_async_copy(src.at[e], dst.at[e], a2a_recv.at[n]).start()

        def near(k, _):
            to = (e + k) % E
            pltpu.make_async_remote_copy(
                src_ref=src.at[to], dst_ref=dst.at[e],
                send_sem=a2a_send.at[n, 0], recv_sem=a2a_recv.at[n],
                device_id=(d, to), device_id_type=MESH,
            ).start()
            return 0

        lax.fori_loop(1, E, near, 0)

    def pack(parts):
        parts = [p.reshape(E, SPE, D) for p in parts]
        return jnp.concatenate(parts, axis=1).astype(BF)

    parts = []
    logits = []
    for i in range(PER):
        lg = dot(images[i], router[...], 1, 0)
        logits.append(lg)
        ex = jnp.exp(lg - jnp.max(lg, axis=0, keepdims=True))
        p = ex / jnp.sum(ex, axis=0, keepdims=True)
        disp[i] = p
        parts.append(dot(p.astype(BF), images[i], 0, 0))
    sb_in[...] = pack(parts)
    pl.semaphore_wait(barrier, 2 * E - 1 + NZ - 1)
    spread(sb_in, x_rows, 0)
    parts = []
    for i in range(PER):
        lg = logits[i]
        ex = jnp.exp(lg - jnp.max(lg, axis=1, keepdims=True))
        p = ex / jnp.sum(ex, axis=1, keepdims=True)
        comb[i] = p
        parts.append(dot(p.astype(BF), out_grad[i], 0, 0))
    sb_grad[...] = pack(parts)
    spread(sb_grad, g_rows, 1)

    def xs():
        return x_rows[...].reshape(2 * ROWS, D)

    def gs():
        return g_rows[...].reshape(2 * ROWS, D)

    def forward(k, _):
        pre = dot(xs(), w_in[k], 1, 0)
        sq = pre * pre
        t = jnp.tanh(pre * (C0 + (C0 * C1) * sq))
        half = 0.5 * pre
        hid[k] = (half + half * t).astype(BF)
        gp[k] = (0.5 + 0.5 * t) + half * ((1.0 - t * t) * (C0 + (3.0 * C0 * C1) * sq))
        return 0

    def backward(k, _):
        dh = dot(gs(), w_out[k], 1, 1)
        da[k] = (dh * gp[k]).astype(BF)
        return 0

    def grad_out(k, _):
        g = dot(hid[k], gs(), 0, 0)
        gw_out[pl.ds(pl.multiple_of(k * TILE, TILE), TILE), :] = g.astype(BF)
        return 0

    def grad_in(k, _):
        g = dot(xt[...], da[k], 1, 0)
        gw_in[:, k] = g.reshape(NZ, CH_IN, TILE).astype(BF)
        return 0

    def rs_copy(which, way, step):
        c = (z + 5 - step) % NZ if way == 0 else (z + 3 + step) % NZ
        if which == 0:
            if step == 1:
                half = CH_OUT // 2
                src = gw_out.at[pl.ds(pl.multiple_of(c * CH_OUT + way * half, 16), half), :]
                dst = ro_half.at[way]
            else:
                src = gw_out.at[pl.ds(pl.multiple_of(c * CH_OUT, 16), CH_OUT), :]
                dst = ro_full.at[way, step - 2]
        else:
            if step == 1:
                src = gw_in.at[c, pl.ds(way * HALF_T, HALF_T)]
                dst = ri_half.at[way]
            else:
                src = gw_in.at[c]
                dst = ri_full.at[way, step - 2]
        return pltpu.make_async_remote_copy(
            src_ref=src, dst_ref=dst,
            send_sem=rs_send.at[which, way, step - 1], recv_sem=rs_recv.at[which, way, step - 1],
            device_id=zdev(1 if way == 0 else NZ - 1), device_id_type=MESH,
        )

    def rs_start(which, step):
        for way in range(2):
            rs_copy(which, way, step).start()

    def rs_next(which, step):
        for way in range(2):
            rs_copy(which, way, step).wait_recv()
            c = (z + 4 - step) % NZ if way == 0 else (z + 4 + step) % NZ
            if which == 0:
                if step == 1:
                    half = CH_OUT // 2
                    rows = pl.ds(pl.multiple_of(c * CH_OUT + way * half, 16), half)
                    got = ro_half[way]
                else:
                    rows = pl.ds(pl.multiple_of(c * CH_OUT, 16), CH_OUT)
                    got = ro_full[way, step - 2]
                gw_out[rows, :] = (gw_out[rows, :].astype(F32) + got.astype(F32)).astype(BF)
            else:
                if step == 1:
                    ks = pl.ds(way * HALF_T, HALF_T)
                    gw_in[c, ks] = (gw_in[c, ks].astype(F32) + ri_half[way].astype(F32)).astype(BF)
                else:
                    gw_in[c] = (gw_in[c].astype(F32) + ri_full[way, step - 2].astype(F32)).astype(BF)
            rs_copy(which, way, step + 1).start()

    def rs_end(which):
        for way in range(2):
            rs_copy(which, way, 4).wait_recv()
        if which == 0:
            rows = pl.ds(pl.multiple_of(z * CH_OUT, 16), CH_OUT)
            total = gw_out[rows, :].astype(F32) + ro_full[0, 2].astype(F32) + ro_full[1, 2].astype(F32)
            w_out_share[...] = total.astype(BF)
        else:
            for k in range(NT):
                t = (HALF_T * pair + k) % NT
                total = gw_in[z, k].astype(F32) + ri_full[0, 2, k].astype(F32) + ri_full[1, 2, k].astype(F32)
                w_in_share[:, pl.ds(pl.multiple_of(t * TILE, TILE), TILE)] = total.astype(BF)

    wait_bytes(x_rows, a2a_recv.at[0])
    for k in range(NT):
        w_copy(k)[0].wait()
    lax.fori_loop(0, HALF_T, forward, 0)
    off = pl.ds(pl.multiple_of(pair * (D // 2), 128), D // 2)
    xt[...] = jnp.transpose(x_rows[:, :, :, off].reshape(2 * ROWS, D // 2))
    wait_bytes(g_rows, a2a_recv.at[1])
    for k in range(NT):
        w_copy(k)[1].wait()
    lax.fori_loop(0, HALF_T, grad_out, 0)
    rs_start(0, 1)
    lax.fori_loop(0, HALF_T, backward, 0)
    rs_next(0, 1)
    lax.fori_loop(HALF_T, NT, forward, 0)
    lax.fori_loop(HALF_T, NT, backward, 0)
    lax.fori_loop(0, NT, grad_in, 0)
    rs_start(1, 1)

    def slot_out(k, acc):
        return acc + dot(hid[k, :ROWS], w_out[k], 1, 0)

    def slot_dx(k, acc):
        return acc + dot(da[k, :ROWS], w_in[k], 1, 1)

    zero = jnp.zeros((ROWS, D), F32)
    so_send[...] = lax.fori_loop(0, NT, slot_out, zero).astype(BF).reshape(E, BLK, D)
    back(so_send, so_home, 2)
    dx_send[...] = lax.fori_loop(0, NT, slot_dx, zero).astype(BF).reshape(E, BLK, D)
    back(dx_send, dx_home, 3)
    rs_next(0, 2)
    rs_next(1, 1)

    def home(ref, i):
        return ref[...].astype(F32).reshape(E, PER, SPE, D)[:, i].reshape(S, D).astype(BF)

    wait_bytes(so_home, a2a_recv.at[2])
    first = []
    for i in range(PER):
        dc = dot(out_grad[i], home(so_home, i), 1, 1)
        cm = comb[i]
        first.append(cm * (dc - jnp.sum(cm * dc, axis=1, keepdims=True)))
    wait_bytes(dx_home, a2a_recv.at[3])
    total = jnp.zeros((S, D), F32)
    for i in range(PER):
        dx = home(dx_home, i)
        dd = dot(images[i], dx, 1, 1)
        dm = disp[i]
        dl = (first[i] + dm * (dd - jnp.sum(dm * dd, axis=0, keepdims=True))).astype(BF)
        total = total + dot(dl, images[i], 0, 0)
        image_grad[i] = (dot(dm.astype(BF), dx, 1, 0) + dot(dl, router[...], 1, 1)).astype(BF)
    rpart[...] = total.reshape(E, SPE, D)

    pltpu.make_async_copy(rpart.at[e], r_a.at[e], ar_recv.at[0]).start()

    def send_a(k, _):
        to = (e + k) % E
        pltpu.make_async_remote_copy(
            src_ref=rpart.at[to], dst_ref=r_a.at[e], send_sem=ar_send.at[0], recv_sem=ar_recv.at[0],
            device_id=(d, to), device_id_type=MESH,
        ).start()
        return 0

    lax.fori_loop(1, E, send_a, 0)
    rs_next(0, 3)
    rs_next(1, 2)
    wait_bytes(r_a, ar_recv.at[0])
    summed = jnp.sum(r_a[...], axis=0)
    b_mine[0] = summed[:, : D // 2]
    b_mine[1] = summed[:, D // 2:]
    b1 = pltpu.make_async_remote_copy(
        src_ref=b_mine.at[1 - pair], dst_ref=r_b1, send_sem=ar_send.at[1], recv_sem=ar_recv.at[1],
        device_id=(other_dp, e), device_id_type=MESH,
    )
    b1.start()
    b1.wait()
    c_mine[...] = b_mine[pair] + r_b1[...]
    b2_self = pltpu.make_async_copy(c_mine, r_b2.at[z], ar_recv.at[2])
    b2_self.start()
    for k in range(1, NZ):
        pltpu.make_async_remote_copy(
            src_ref=c_mine, dst_ref=r_b2.at[z], send_sem=ar_send.at[2], recv_sem=ar_recv.at[2],
            device_id=zdev(k), device_id_type=MESH,
        ).start()
    rs_next(1, 3)
    rs_end(0)
    wait_bytes(r_b2, ar_recv.at[2])
    wait_bytes(r_b2.at[pl.ds(0, NZ - 1)], ar_send.at[2])
    c_mine[...] = jnp.sum(r_b2[...], axis=0)
    pltpu.make_async_copy(c_mine, r_c.at[pair, e], ar_recv.at[3]).start()

    def send_c_far(k, _):
        pltpu.make_async_remote_copy(
            src_ref=c_mine, dst_ref=r_c.at[pair, e], send_sem=ar_send.at[3], recv_sem=ar_recv.at[3],
            device_id=(other_dp, (e + k) % E), device_id_type=MESH,
        ).start()
        return 0

    def send_c(k, _):
        pltpu.make_async_remote_copy(
            src_ref=c_mine, dst_ref=r_c.at[pair, e], send_sem=ar_send.at[4], recv_sem=ar_recv.at[3],
            device_id=(d, (e + k) % E), device_id_type=MESH,
        ).start()
        return send_c_far(k, 0)

    send_c_far(0, 0)
    lax.fori_loop(1, E, send_c, 0)
    rs_end(1)
    wait_bytes(r_c, ar_recv.at[3])
    for h in range(2):
        router_grad_t[:, h * (D // 2): (h + 1) * (D // 2)] = r_c[h].reshape(S, D // 2)

    for n in range(2):
        wait_bytes(sb_in.at[pl.ds(0, E - 1)], a2a_send.at[n, 0])
        wait_bytes(sb_in, a2a_send.at[n, 1])
    for n in range(2, 4):
        wait_bytes(so_send.at[pl.ds(0, E - 1)], a2a_send.at[n, 0])
    for which in range(2):
        for way in range(2):
            for step in range(1, 5):
                rs_copy(which, way, step).wait_send()
    wait_bytes(rpart.at[pl.ds(0, E - 1)], ar_send.at[0])
    wait_bytes(r_c.at[0], ar_send.at[3])
    wait_bytes(r_c.at[0, pl.ds(0, E - 1)], ar_send.at[4])


def local(images, out_grad, router, w_in, w_out):
    vm = pl.BlockSpec(memory_space=pltpu.VMEM)
    hbm = pl.BlockSpec(memory_space=pl.ANY)
    V = pltpu.VMEM
    image_grad, router_grad_t, w_in_share, w_out_share = pl.pallas_call(
        kernel,
        out_shape=(
            jax.ShapeDtypeStruct((PER, M, D), BF),
            jax.ShapeDtypeStruct((S, D), F32),
            jax.ShapeDtypeStruct((CH_IN, H), BF),
            jax.ShapeDtypeStruct((CH_OUT, D), BF),
        ),
        in_specs=[vm, vm, vm, hbm, hbm],
        out_specs=(vm, vm, vm, vm),
        scratch_shapes=[
            V((NT, D, TILE), BF), V((NT, TILE, D), BF),
            V((PER, M, S), F32), V((PER, M, S), F32),
            V((E, BLK, D), BF), V((E, BLK, D), BF),
            V((2, E, BLK, D), BF), V((2, E, BLK, D), BF),
            V((NT, 2 * ROWS, TILE), BF), V((NT, 2 * ROWS, TILE), F32), V((NT, 2 * ROWS, TILE), BF),
            V((D // 2, 2 * ROWS), BF),
            V((H // 2, D), BF), V((NZ, NT, CH_IN, TILE), BF),
            V((2, CH_OUT // 2, D), BF), V((2, 3, CH_OUT, D), BF),
            V((2, HALF_T, CH_IN, TILE), BF), V((2, 3, NT, CH_IN, TILE), BF),
            V((E, BLK, D), BF), V((E, BLK, D), BF), V((E, BLK, D), BF), V((E, BLK, D), BF),
            V((E, SPE, D), F32), V((E, SPE, D), F32),
            V((SPE, D // 2), F32), V((2, SPE, D // 2), F32), V((NZ, SPE, D // 2), F32), V((SPE, D // 2), F32),
            V((2, E, SPE, D // 2), F32),
            pltpu.SemaphoreType.DMA((2, NT)),
            pltpu.SemaphoreType.DMA((4, 2)), pltpu.SemaphoreType.DMA((4,)),
            pltpu.SemaphoreType.DMA((2, 2, 4)), pltpu.SemaphoreType.DMA((2, 2, 4)),
            pltpu.SemaphoreType.DMA((5,)), pltpu.SemaphoreType.DMA((4,)),
            pltpu.SemaphoreType.DMA((1,)),
        ],
        compiler_params=pltpu.CompilerParams(
            collective_id=0, has_side_effects=True, vmem_limit_bytes=60 * 1024 * 1024
        ),
    )(images, out_grad, router, w_in[0], w_out[0])
    return image_grad, router_grad_t.T, w_in_share[None], w_out_share[None]


def solution(mesh):
    return jax.shard_map(
        local,
        mesh=mesh,
        in_specs=(
            P(("dp", "expert"), None, None),
            P(("dp", "expert"), None, None),
            P(),
            P("expert", None, None),
            P("expert", None, None),
        ),
        out_specs=(
            P(("dp", "expert"), None, None),
            P(),
            P("expert", "dp", None),
            P("expert", "dp", None),
        ),
        check_vma=False,
    )
```

time: 369 us -> 100 us (0.27)
  waiting for transfers between devices: 271 us -> 0 us
  Pallas kernels: 0 us -> 92.1 us
  matrix products: 43 us -> 0 us
  starting transfers between devices: 25 us -> 0 us
  between operations: 15.6 us -> 0.64 us
    psum x1 -> x0, waiting for transfers between devices: 247 us -> none  [local(): router_grad = lax.psum(router_part, ('dp', 'expert'))]
    pallas_call x0 -> x1, Pallas kernels: none -> 92.1 us  [local(): pl.pallas_call(kernel, out_shape=(jax.ShapeDtypeStruct((PER, M, D), BF),...]
    dot_general x14 -> x0, matrix products: 43 us -> none  [the longest x2 10.6 us: contract_last(): lax.dot_general(left, right, (((1,), (1,)), ((), ())), preferred_element_...]
    all_to_all x4 -> x0, starting transfers between devices: 24.7 us -> none  [the longest x1 8.45 us: local(): lax.all_to_all(slot_grad, 'expert', split_axis=1, concat_axis=0, tiled=True)]
    all_to_all x4 -> x0, waiting for transfers between devices: 24.3 us -> none  [the longest x1 9.16 us: local(): lax.all_to_all(slot_in, 'expert', split_axis=1, concat_axis=0, tiled=True)]
  transfers between devices with their start and end apart: 7 -> 0, of which waited for: 4 -> 0; matrix products, arithmetic and copies ran while one was open for 9% -> 0% of each run, Pallas kernels for 0% -> 0%
where the time goes in v1:
time: 100 us
  Pallas kernels  92.1 us (92%)
  local copies, waits for them, and re-layouts  7.36 us (7%)
    pallas_call x1, Pallas kernels, local(): pl.pallas_call(kernel, out_shape=(jax.ShapeDtypeStruct((PER, M, D), BF),...  92.1 us
    unnamed x4, local copies, waits for them, and re-layouts  7.36 us

profile of v1, /device:TPU:1, one launch (start us, length us, event | category | flops | bytes accessed | tf_op | source)
XLA Modules:
  0.0 100.1 jit_solution(1599882825182101107)
XLA Ops:
  0.6 92.1 %shard_map.84 = (bf16[2,256,768]{2,1,0:T(8,128)(2,1)}, f32[128,768]{1,0:T(8,128)}, bf16[48,3072]{1,0:T(8,128)(2,1)}, bf16[192,768]{1,0:T(8,128)(2,1)}) custom-call(bf16[2,256,768]{2,1,0:T(8,128)(2,1)} %images.1, bf16[2,256,768]{2,1,0:T(8,128)(2,1)} %out_grad.1, bf16[768,128]{1,0:T(8,128)(2,1)} %router.1, bf16[768,3072]{1,0:T(8,128)(2,1)} %bitcast.5, ...), custom_call_target="tpu_custom_call" | custom-call | tf_op jit(solution)/shard_map/pallas_call | solution.py:371
  92.7 1.9 %copy.9 = f32[768,128]{1,0:T(8,128)} copy(f32[768,128]{0,1:T(8,128)} %bitcast.7) | data formatting | bytes 786432
  94.6 2.1 %copy.13 = bf16[2,256,768]{2,1,0:T(8,128)(2,1)} copy(bf16[2,256,768]{2,1,0:T(8,128)(2,1)} %get-tuple-element.20) | data formatting | bytes 1572864
  96.7 1.7 %copy.14 = bf16[1,48,3072]{2,1,0:T(8,128)(2,1)} copy(bf16[1,48,3072]{2,1,0:T(8,128)(2,1)} %bitcast.9) | data formatting | bytes 589824
  98.4 1.7 %copy.15 = bf16[1,192,768]{2,1,0:T(8,128)(2,1)} copy(bf16[1,192,768]{2,1,0:T(8,128)(2,1)} %bitcast.8) | data formatting | bytes 589824

commit v2 on v1

v2 whole, which is shorter than its diff:
```python
import math

import jax
import jax.numpy as jnp
from jax import lax
from jax.experimental import pallas as pl
from jax.experimental.pallas import tpu as pltpu
from jax.sharding import PartitionSpec as P

MESH = pl.DeviceIdType.MESH
BF = jnp.bfloat16
F32 = jnp.float32

D = 768
H = 3072
M = 256
S = 128
E = 16
NZ = 8
PER = 2
SPE = 8
BLK = PER * SPE
ROWS = E * BLK
TILE = 768
NT = H // TILE
HALF_T = NT // 2
IN_FLIGHT = 4
CH_IN = D // (2 * NZ)
CH_OUT = H // (2 * NZ)
C0 = math.sqrt(2.0 / math.pi)
C1 = 0.044715


def dot(a, b, ca, cb):
    return lax.dot_general(a, b, (((ca,), (cb,)), ((), ())), preferred_element_type=F32)


def kernel(
    images_hbm, out_grad_hbm, router_hbm, w_in_hbm, w_out_hbm,
    image_grad_hbm, router_grad_hbm, w_in_share_hbm, w_out_share_hbm,
    images, out_grad, router, image_grad, router_grad_t, w_in_share, w_out_share,
    w_in, w_out, disp, comb, sb_in, sb_grad, x_rows, g_rows,
    hid, gp, da, xt, gw_out, gw_in,
    ro_half, ro_full, ri_half, ri_full,
    so_send, dx_send, so_home, dx_home,
    rpart, r_a, b_rows, r_b2, c_row, r_b3, c_mine, r_c,
    w_sem, io_sem, a2a_send, a2a_recv, rs_send, rs_recv, ar_send, ar_recv,
):
    d = lax.axis_index("dp")
    e = lax.axis_index("expert")
    pair = d // NZ
    z = d % NZ
    other_dp = (1 - pair) * NZ + z

    def zdev(k):
        return (pair * NZ + (z + k) % NZ, e)

    def zdev_other(k):
        return ((1 - pair) * NZ + (z + k) % NZ, e)

    barrier = pltpu.get_barrier_semaphore()

    def greet(k, _):
        pl.semaphore_signal(barrier, inc=1, device_id=(other_dp, (e + k) % E), device_id_type=MESH)
        return 0

    def greet_own(k, _):
        pl.semaphore_signal(barrier, inc=1, device_id=(d, (e + k) % E), device_id_type=MESH)
        return 0

    lax.fori_loop(0, E, greet, 0)
    lax.fori_loop(1, E, greet_own, 0)
    for k in range(1, NZ):
        pl.semaphore_signal(barrier, inc=1, device_id=zdev(k), device_id_type=MESH)
        pl.semaphore_signal(barrier, inc=1, device_id=zdev_other(k), device_id_type=MESH)

    inputs = [
        pltpu.make_async_copy(images_hbm, images, io_sem.at[0]),
        pltpu.make_async_copy(router_hbm, router, io_sem.at[1]),
        pltpu.make_async_copy(out_grad_hbm, out_grad, io_sem.at[2]),
    ]
    for c in inputs:
        c.start()

    def tile_of(k):
        return 2 * ((pair + k // 2) % 2) + (1 - z // 4 + k) % 2

    def w_in_copy(k):
        cols = pl.ds(pl.multiple_of(tile_of(k) * TILE, TILE), TILE)
        return pltpu.make_async_copy(w_in_hbm.at[:, cols], w_in.at[k], w_sem.at[0, k])

    def w_out_copy(k):
        rows = pl.ds(pl.multiple_of(tile_of(k) * TILE, TILE), TILE)
        return pltpu.make_async_copy(w_out_hbm.at[rows, :], w_out.at[k], w_sem.at[1, k])

    for k in range(NT):
        w_in_copy(k).start()
    for k in range(NT):
        w_out_copy(k).start()

    def spread(src, dst, n):
        pltpu.make_async_copy(src.at[e], dst.at[0, e], a2a_recv.at[n]).start()

        def far(k, _):
            to = (e + k) % E
            pltpu.make_async_remote_copy(
                src_ref=src.at[to], dst_ref=dst.at[1, e],
                send_sem=a2a_send.at[n, 1], recv_sem=a2a_recv.at[n + 4],
                device_id=(other_dp, to), device_id_type=MESH,
            ).start()
            return 0

        def both(k, _):
            to = (e + k) % E
            pltpu.make_async_remote_copy(
                src_ref=src.at[to], dst_ref=dst.at[0, e],
                send_sem=a2a_send.at[n, 0], recv_sem=a2a_recv.at[n],
                device_id=(d, to), device_id_type=MESH,
            ).start()
            return far(k, 0)

        far(0, 0)
        lax.fori_loop(1, E, both, 0)

    def wait_bytes(ref, sem):
        pltpu.make_async_copy(ref, ref, sem).wait()

    def back(src, dst, n):
        pltpu.make_async_copy(src.at[e], dst.at[e], a2a_recv.at[n]).start()

        def near(k, _):
            to = (e + k) % E
            pltpu.make_async_remote_copy(
                src_ref=src.at[to], dst_ref=dst.at[e],
                send_sem=a2a_send.at[n, 0], recv_sem=a2a_recv.at[n],
                device_id=(d, to), device_id_type=MESH,
            ).start()
            return 0

        lax.fori_loop(1, E, near, 0)

    def pack(parts):
        parts = [p.reshape(E, SPE, D) for p in parts]
        return jnp.concatenate(parts, axis=1).astype(BF)

    parts = []
    logits = []
    inputs[0].wait()
    inputs[1].wait()
    for i in range(PER):
        lg = dot(images[i], router[...], 1, 0)
        logits.append(lg)
        ex = jnp.exp(lg - jnp.max(lg, axis=0, keepdims=True))
        p = ex / jnp.sum(ex, axis=0, keepdims=True)
        disp[i] = p
        parts.append(dot(p.astype(BF), images[i], 0, 0))
    sb_in[...] = pack(parts)
    pl.semaphore_wait(barrier, 2 * E - 1 + 2 * (NZ - 1))
    spread(sb_in, x_rows, 0)
    inputs[2].wait()
    parts = []
    for i in range(PER):
        lg = logits[i]
        ex = jnp.exp(lg - jnp.max(lg, axis=1, keepdims=True))
        p = ex / jnp.sum(ex, axis=1, keepdims=True)
        comb[i] = p
        parts.append(dot(p.astype(BF), out_grad[i], 0, 0))
    sb_grad[...] = pack(parts)
    wait_bytes(sb_in.at[pl.ds(0, E - 1)], a2a_send.at[0, 0])
    wait_bytes(sb_in, a2a_send.at[0, 1])
    spread(sb_grad, g_rows, 1)

    def xs():
        return x_rows[...].reshape(2 * ROWS, D)

    def forward(k, _):
        w_in_copy(k).wait()
        pre = dot(xs(), w_in[k], 1, 0)
        sq = pre * pre
        t = jnp.tanh(pre * (C0 + (C0 * C1) * sq))
        half = 0.5 * pre
        hid[k] = (half + half * t).astype(BF)
        gp[k] = (0.5 + 0.5 * t) + half * ((1.0 - t * t) * (C0 + (3.0 * C0 * C1) * sq))
        return 0

    def grad_out(k):
        g = dot(hid[k], g_rows[...].reshape(2 * ROWS, D), 0, 0).astype(BF)
        gw_out[pl.ds(((1 - z // 4 + k) % 2) * (NZ // 2), NZ // 2)] = g.reshape(NZ // 2, CH_OUT, D)

    def backward(k, part):
        rows = pl.ds(part * ROWS, ROWS)
        dh = dot(g_rows[part].reshape(ROWS, D), w_out[k], 1, 1)
        da[k, rows] = (dh * gp[k, rows]).astype(BF)

    def backward_own(k, _):
        backward(k, 0)
        return 0

    def grad_in(k, _):
        backward(k, 1)
        g = dot(xt[...], da[k], 1, 0)
        gw_in[:, tile_of(k)] = g.reshape(NZ, CH_IN, TILE).astype(BF)
        return 0

    def piece(which, part, c, way=None):
        if which == 0:
            rows = CH_OUT // 2 if way is None else CH_OUT // 4
            return (c, pl.ds(part * (CH_OUT // 2) + (way or 0) * rows, rows))
        first = HALF_T * ((pair + part) % 2)
        return (c, pl.ds(first, HALF_T)) if way is None else (c, pl.ds(first + way, 1))

    def rs_copy(which, part, way, step):
        c = (z + 5 - step) % NZ if way == 0 else (z + 3 + step) % NZ
        mine, half, full = ((gw_out, ro_half, ro_full), (gw_in, ri_half, ri_full))[which]
        src = mine.at[piece(which, part, c, way if step == 1 else None)]
        dst = half.at[part, way] if step == 1 else full.at[part, way, step - 2]
        return pltpu.make_async_remote_copy(
            src_ref=src, dst_ref=dst,
            send_sem=rs_send.at[which, part, way, step - 1], recv_sem=rs_recv.at[which, part, way, step - 1],
            device_id=zdev(1 if way == 0 else NZ - 1), device_id_type=MESH,
        )

    sent = []

    def rs_send_on(which, part, way, step):
        n = len(sent) // 2 - IN_FLIGHT
        if n >= 0:
            rs_copy(*sent[2 * n + way]).wait_send()
        rs_copy(which, part, way, step).start()
        sent.append((which, part, way, step))

    def rs_start(which, part):
        for way in range(2):
            rs_send_on(which, part, way, 1)

    def rs_next(which, part, step):
        mine, half, full = ((gw_out, ro_half, ro_full), (gw_in, ri_half, ri_full))[which]
        for way in range(2):
            rs_copy(which, part, way, step).wait_recv()
            c = (z + 4 - step) % NZ if way == 0 else (z + 4 + step) % NZ
            here = piece(which, part, c, way if step == 1 else None)
            got = half[part, way] if step == 1 else full[part, way, step - 2]
            mine[here] = (mine[here].astype(F32) + got.astype(F32)).astype(BF)
            rs_send_on(which, part, way, step + 1)

    def rs_end(which, part):
        for way in range(2):
            rs_copy(which, part, way, 4).wait_recv()
        if which == 0:
            rows = slice(part * (CH_OUT // 2), (part + 1) * (CH_OUT // 2))
            got = ro_full[part, 0, 2].astype(F32) + ro_full[part, 1, 2].astype(F32)
            w_out_share[rows, :] = (gw_out[z, rows, :].astype(F32) + got).astype(BF)
        else:
            for n in range(HALF_T):
                t = HALF_T * ((pair + part) % 2) + n
                got = ri_full[part, 0, 2, n].astype(F32) + ri_full[part, 1, 2, n].astype(F32)
                cols = pl.ds(pl.multiple_of(t * TILE, TILE), TILE)
                w_in_share[:, cols] = (gw_in[z, t].astype(F32) + got).astype(BF)

    wait_bytes(x_rows.at[0], a2a_recv.at[0])
    wait_bytes(x_rows.at[1], a2a_recv.at[4])
    lax.fori_loop(0, NT, forward, 0)
    off = pl.ds(pl.multiple_of(pair * (D // 2), 128), D // 2)
    xt[...] = jnp.transpose(x_rows[:, :, :, off].reshape(2 * ROWS, D // 2))
    acc = None
    for k in range(NT):
        w_out_copy(k).wait()
        part = dot(hid[k, :ROWS], w_out[k], 1, 0)
        acc = part if acc is None else acc + part
    so_send[...] = acc.astype(BF).reshape(E, BLK, D)
    wait_bytes(g_rows.at[0], a2a_recv.at[1])
    wait_bytes(g_rows.at[1], a2a_recv.at[5])
    grad_out(0)
    rs_start(0, 0)
    rs_start(0, 1)
    back(so_send, so_home, 2)
    grad_out(1)
    lax.fori_loop(0, NT, backward_own, 0)
    acc = dot(da[0, :ROWS], w_in[0], 1, 1)
    for k in range(1, NT):
        acc = acc + dot(da[k, :ROWS], w_in[k], 1, 1)
    dx_send[...] = acc.astype(BF).reshape(E, BLK, D)
    back(dx_send, dx_home, 3)
    rs_next(0, 0, 1)
    rs_next(0, 1, 1)
    lax.fori_loop(0, HALF_T, grad_in, 0)
    rs_start(1, 0)
    lax.fori_loop(HALF_T, NT, grad_in, 0)
    rs_start(1, 1)
    rs_next(0, 0, 2)
    rs_next(1, 0, 1)

    def home(ref, i):
        return ref[...].astype(F32).reshape(E, PER, SPE, D)[:, i].reshape(S, D).astype(BF)

    wait_bytes(so_home, a2a_recv.at[2])
    first = []
    for i in range(PER):
        dc = dot(out_grad[i], home(so_home, i), 1, 1)
        cm = comb[i]
        first.append(cm * (dc - jnp.sum(cm * dc, axis=1, keepdims=True)))
    wait_bytes(dx_home, a2a_recv.at[3])
    total = jnp.zeros((S, D), F32)
    for i in range(PER):
        dx = home(dx_home, i)
        dd = dot(images[i], dx, 1, 1)
        dm = disp[i]
        dl = (first[i] + dm * (dd - jnp.sum(dm * dd, axis=0, keepdims=True))).astype(BF)
        total = total + dot(dl, images[i], 0, 0)
        image_grad[i] = (dot(dm.astype(BF), dx, 1, 0) + dot(dl, router[...], 1, 1)).astype(BF)
    rpart[...] = total.reshape(E, SPE, D)
    image_grad_out = pltpu.make_async_copy(image_grad, image_grad_hbm, io_sem.at[3])
    image_grad_out.start()

    pltpu.make_async_copy(rpart.at[e], r_a.at[e], ar_recv.at[0]).start()

    def send_a(k, _):
        to = (e + k) % E
        pltpu.make_async_remote_copy(
            src_ref=rpart.at[to], dst_ref=r_a.at[e], send_sem=ar_send.at[0], recv_sem=ar_recv.at[0],
            device_id=(d, to), device_id_type=MESH,
        ).start()
        return 0

    lax.fori_loop(1, E, send_a, 0)
    rs_next(1, 1, 1)
    rs_next(0, 1, 2)
    rs_next(1, 0, 2)
    wait_bytes(r_a, ar_recv.at[0])
    summed = jnp.sum(r_a[...], axis=0)
    for h in range(2):
        for r in range(NZ):
            b_rows[h, r] = summed[r:r + 1, h * (D // 2): (h + 1) * (D // 2)]
    pltpu.make_async_copy(b_rows.at[pair, z], r_b2.at[pair, z], ar_recv.at[2]).start()
    for k in range(NZ):
        to = (z + k) % NZ
        if k:
            pltpu.make_async_remote_copy(
                src_ref=b_rows.at[pair, to], dst_ref=r_b2.at[pair, z], send_sem=ar_send.at[2], recv_sem=ar_recv.at[2],
                device_id=zdev(k), device_id_type=MESH,
            ).start()
        pltpu.make_async_remote_copy(
            src_ref=b_rows.at[1 - pair, to], dst_ref=r_b2.at[pair, z], send_sem=ar_send.at[1], recv_sem=ar_recv.at[2],
            device_id=zdev_other(k), device_id_type=MESH,
        ).start()
    rs_next(1, 1, 2)
    wait_bytes(r_b2, ar_recv.at[2])
    c_row[0] = jnp.sum(r_b2[...].reshape(2 * NZ, 1, D // 2), axis=0)
    pltpu.make_async_copy(c_row.at[0], r_b3.at[z], ar_recv.at[4]).start()
    for k in range(1, NZ):
        pltpu.make_async_remote_copy(
            src_ref=c_row.at[0], dst_ref=r_b3.at[z], send_sem=ar_send.at[5], recv_sem=ar_recv.at[4],
            device_id=zdev(k), device_id_type=MESH,
        ).start()
    rs_next(0, 0, 3)
    wait_bytes(r_b3, ar_recv.at[4])
    for r in range(NZ):
        c_mine[r:r + 1, :] = r_b3[r]
    pltpu.make_async_copy(c_mine, r_c.at[pair, e], ar_recv.at[3]).start()

    def send_c_far(k, _):
        pltpu.make_async_remote_copy(
            src_ref=c_mine, dst_ref=r_c.at[pair, e], send_sem=ar_send.at[3], recv_sem=ar_recv.at[3],
            device_id=(other_dp, (e + k) % E), device_id_type=MESH,
        ).start()
        return 0

    def send_c(k, _):
        pltpu.make_async_remote_copy(
            src_ref=c_mine, dst_ref=r_c.at[pair, e], send_sem=ar_send.at[4], recv_sem=ar_recv.at[3],
            device_id=(d, (e + k) % E), device_id_type=MESH,
        ).start()
        return send_c_far(k, 0)

    send_c_far(0, 0)
    lax.fori_loop(1, E, send_c, 0)
    rs_next(0, 1, 3)
    rs_next(1, 0, 3)
    rs_next(1, 1, 3)
    outputs = [
        pltpu.make_async_copy(router_grad_t, router_grad_hbm, io_sem.at[4]),
        pltpu.make_async_copy(w_out_share, w_out_share_hbm, io_sem.at[5]),
        pltpu.make_async_copy(w_in_share, w_in_share_hbm, io_sem.at[6]),
    ]
    rs_end(0, 0)
    rs_end(0, 1)
    outputs[1].start()
    rs_end(1, 0)
    wait_bytes(r_c, ar_recv.at[3])
    for h in range(2):
        router_grad_t[:, h * (D // 2): (h + 1) * (D // 2)] = r_c[h].reshape(S, D // 2)
    outputs[0].start()
    rs_end(1, 1)
    outputs[2].start()

    wait_bytes(sb_grad.at[pl.ds(0, E - 1)], a2a_send.at[1, 0])
    wait_bytes(sb_grad, a2a_send.at[1, 1])
    for n in range(2, 4):
        wait_bytes(so_send.at[pl.ds(0, E - 1)], a2a_send.at[n, 0])
    for last in sent[-2 * IN_FLIGHT:]:
        rs_copy(*last).wait_send()
    wait_bytes(rpart.at[pl.ds(0, E - 1)], ar_send.at[0])
    wait_bytes(b_rows.at[0], ar_send.at[1])
    for n in (2, 5):
        wait_bytes(b_rows.at[0, pl.ds(0, NZ - 1)], ar_send.at[n])
    wait_bytes(r_c.at[0], ar_send.at[3])
    wait_bytes(r_c.at[0, pl.ds(0, E - 1)], ar_send.at[4])
    image_grad_out.wait()
    for c in outputs:
        c.wait()


def deliver(image_grad_in, router_grad_in, w_in_in, w_out_in, image_grad, router_grad, w_in_share, w_out_share,
            held, held_in, held_out, router_t, router_held, sem):
    steps = (
        (router_grad_in, router_t, None),
        (image_grad_in, held, image_grad),
        (w_in_in, held_in, w_in_share.at[0]),
        (w_out_in, held_out, w_out_share.at[0]),
    )
    first = [pltpu.make_async_copy(a, b, sem.at[0, n]) for n, (a, b, _) in enumerate(steps)]
    second = [
        pltpu.make_async_copy(router_held, router_grad, sem.at[1, 0]),
        *(pltpu.make_async_copy(b, c, sem.at[1, n + 1]) for n, (_, b, c) in enumerate(steps[1:])),
    ]
    for c in first:
        c.start()
    first[0].wait()
    router_held[...] = jnp.transpose(router_t[...])
    second[0].start()
    for c, after in zip(first[1:], second[1:]):
        c.wait()
        after.start()
    for c in second:
        c.wait()


def local(images, out_grad, router, w_in, w_out):
    hbm = pl.BlockSpec(memory_space=pltpu.HBM)
    V = pltpu.VMEM
    DMA = pltpu.SemaphoreType.DMA
    parts = pl.pallas_call(
        kernel,
        out_shape=(
            jax.ShapeDtypeStruct((PER, M, D), BF),
            jax.ShapeDtypeStruct((S, D), F32),
            jax.ShapeDtypeStruct((CH_IN, H), BF),
            jax.ShapeDtypeStruct((CH_OUT, D), BF),
        ),
        in_specs=[hbm] * 5,
        out_specs=(hbm,) * 4,
        scratch_shapes=[
            V((PER, M, D), BF), V((PER, M, D), BF), V((D, S), BF),
            V((PER, M, D), BF), V((S, D), F32), V((CH_IN, H), BF), V((CH_OUT, D), BF),
            V((NT, D, TILE), BF), V((NT, TILE, D), BF),
            V((PER, M, S), F32), V((PER, M, S), F32),
            V((E, BLK, D), BF), V((E, BLK, D), BF),
            V((2, E, BLK, D), BF), V((2, E, BLK, D), BF),
            V((NT, 2 * ROWS, TILE), BF), V((NT, 2 * ROWS, TILE), F32), V((NT, 2 * ROWS, TILE), BF),
            V((D // 2, 2 * ROWS), BF),
            V((NZ, CH_OUT, D), BF), V((NZ, NT, CH_IN, TILE), BF),
            V((2, 2, CH_OUT // 4, D), BF), V((2, 2, 3, CH_OUT // 2, D), BF),
            V((2, 2, 1, CH_IN, TILE), BF), V((2, 2, 3, HALF_T, CH_IN, TILE), BF),
            V((E, BLK, D), BF), V((E, BLK, D), BF), V((E, BLK, D), BF), V((E, BLK, D), BF),
            V((E, SPE, D), F32), V((E, SPE, D), F32),
            V((2, NZ, 1, D // 2), F32), V((2, NZ, 1, D // 2), F32),
            V((1, 1, D // 2), F32), V((NZ, 1, D // 2), F32), V((SPE, D // 2), F32),
            V((2, E, SPE, D // 2), F32),
            DMA((2, NT)), DMA((7,)),
            DMA((4, 2)), DMA((6,)),
            DMA((2, 2, 2, 4)), DMA((2, 2, 2, 4)),
            DMA((6,)), DMA((5,)),
        ],
        compiler_params=pltpu.CompilerParams(
            collective_id=0, has_side_effects=True, vmem_limit_bytes=60 * 1024 * 1024
        ),
    )(images, out_grad, router, w_in[0], w_out[0])
    return pl.pallas_call(
        deliver,
        out_shape=(
            jax.ShapeDtypeStruct((PER, M, D), BF),
            jax.ShapeDtypeStruct((D, S), F32),
            jax.ShapeDtypeStruct((1, CH_IN, H), BF),
            jax.ShapeDtypeStruct((1, CH_OUT, D), BF),
        ),
        in_specs=[hbm] * 4,
        out_specs=(hbm,) * 4,
        scratch_shapes=[
            V((PER, M, D), BF), V((CH_IN, H), BF), V((CH_OUT, D), BF), V((S, D), F32), V((D, S), F32), DMA((2, 4)),
        ],
        compiler_params=pltpu.CompilerParams(vmem_limit_bytes=60 * 1024 * 1024),
    )(*parts)


def solution(mesh):
    return jax.shard_map(
        local,
        mesh=mesh,
        in_specs=(
            P(("dp", "expert"), None, None),
            P(("dp", "expert"), None, None),
            P(),
            P("expert", None, None),
            P("expert", None, None),
        ),
        out_specs=(
            P(("dp", "expert"), None, None),
            P(),
            P("expert", "dp", None),
            P("expert", "dp", None),
        ),
        check_vma=False,
    )
```

time: 100 us -> 86.7 us (0.87)
  the two profiles are of different devices: /device:TPU:1 before, /device:TPU:8 now
where the time goes in v2:
time: 86.7 us; the launch traced here: 86.6 us
  Pallas kernels  86 us (99%)
    pallas_call x1, Pallas kernels, local(): pl.pallas_call(kernel, out_shape=(jax.ShapeDtypeStruct((PER, M, D), BF),...  83.6 us
    pallas_call x1, Pallas kernels, local(): pl.pallas_call(deliver, out_shape=(jax.ShapeDtypeStruct((PER, M, D), BF),...  2.43 us

profile of v2, /device:TPU:8, one launch (start us, length us, event | category | flops | bytes accessed | tf_op | source)
XLA Modules:
  0.0 86.6 jit_solution(730124825559350583)
XLA Ops:
  0.6 83.6 %shard_map.84 = (bf16[2,256,768]{2,1,0:T(8,128)(2,1)}, f32[128,768]{1,0:T(8,128)}, bf16[48,3072]{1,0:T(8,128)(2,1)}, bf16[192,768]{1,0:T(8,128)(2,1)}) custom-call(bf16[2,256,768]{2,1,0:T(8,128)(2,1)} %images_hbm.1, bf16[2,256,768]{2,1,0:T(8,128)(2,1)} %out_grad_hbm.1, bf16[768,128]{1,0:T(8,128)(2,1)} %router_hbm.1, bf16[768,3072]{1,0:T(8,128)(2,1)} %bitcast.2, ...), custom_call_target="tpu_custom_call" | custom-call | tf_op jit(solution)/shard_map/pallas_call | solution.py:442
  84.2 2.4 %shard_map.85 = (bf16[2,256,768]{2,1,0:T(8,128)(2,1)}, f32[768,128]{1,0:T(8,128)}, bf16[1,48,3072]{2,1,0:T(8,128)(2,1)}, bf16[1,192,768]{2,1,0:T(8,128)(2,1)}) custom-call(bf16[2,256,768]{2,1,0:T(8,128)(2,1)} %get-tuple-element.8.image_grad_in, f32[128,768]{1,0:T(8,128)} %get-tuple-element.9.router_grad_in, bf16[48,3072]{1,0:T(8,128)(2,1)} %get-tuple-element.10.w_in_in, ...), custom_call_target="tpu_custom_call" | custom-call | tf_op jit(solution)/shard_map/pallas_call | solution.py:478

commit v3 on v2

v3 whole, which is shorter than its diff:
```python
import math

import jax
import jax.numpy as jnp
from jax import lax
from jax.experimental import pallas as pl
from jax.experimental.pallas import tpu as pltpu
from jax.sharding import PartitionSpec as P

MESH = pl.DeviceIdType.MESH
BF = jnp.bfloat16
F32 = jnp.float32

D = 768
H = 3072
M = 256
S = 128
E = 16
NZ = 8
PER = 2
SPE = 8
BLK = PER * SPE
ROWS = E * BLK
TILE = 768
NT = H // TILE
HALF_T = NT // 2
GP = 3
GW = D // GP
IN_FLIGHT = 5
CH_IN = D // (2 * NZ)
CH_OUT = H // (2 * NZ)
C0 = math.sqrt(2.0 / math.pi)
C1 = 0.044715


def dot(a, b, ca, cb):
    return lax.dot_general(a, b, (((ca,), (cb,)), ((), ())), preferred_element_type=F32)


def kernel(
    images_hbm, out_grad_hbm, router_hbm, w_in_hbm, w_out_hbm,
    image_grad, router_grad, w_in_share, w_out_share,
    images, out_grad, router,
    w_in, w_out, disp, comb, sb_in, sb_grad, x_rows, g_rows,
    hid, hid_t, gp, da, xt, gw_out, gw_in,
    ro_half, ro_full, ri_half, ri_full,
    so_send, dx_send, so_home, dx_home,
    rpart, r_a, b_rows, r_b2, c_row, r_b3, c_mine, r_c,
    w_sem, io_sem, a2a_send, a2a_recv, rs_send, rs_recv, ar_send, ar_recv,
):
    d = lax.axis_index("dp")
    e = lax.axis_index("expert")
    pair = d // NZ
    z = d % NZ
    other_dp = (1 - pair) * NZ + z

    def zdev(k):
        return (pair * NZ + (z + k) % NZ, e)

    def zdev_other(k):
        return ((1 - pair) * NZ + (z + k) % NZ, e)

    barrier = pltpu.get_barrier_semaphore()

    def greet(k, _):
        pl.semaphore_signal(barrier, inc=1, device_id=(other_dp, (e + k) % E), device_id_type=MESH)
        return 0

    def greet_own(k, _):
        pl.semaphore_signal(barrier, inc=1, device_id=(d, (e + k) % E), device_id_type=MESH)
        return 0

    lax.fori_loop(0, E, greet, 0)
    lax.fori_loop(1, E, greet_own, 0)
    for k in range(1, NZ):
        pl.semaphore_signal(barrier, inc=1, device_id=zdev(k), device_id_type=MESH)
        pl.semaphore_signal(barrier, inc=1, device_id=zdev_other(k), device_id_type=MESH)

    inputs = [
        pltpu.make_async_copy(images_hbm, images, io_sem.at[0]),
        pltpu.make_async_copy(router_hbm, router, io_sem.at[1]),
        pltpu.make_async_copy(out_grad_hbm, out_grad, io_sem.at[2]),
    ]
    for c in inputs:
        c.start()

    def tile_of(k):
        return 2 * ((pair + k // 2) % 2) + (1 - z // 4 + k) % 2

    def w_in_copy(k):
        cols = pl.ds(pl.multiple_of(tile_of(k) * TILE, TILE), TILE)
        return pltpu.make_async_copy(w_in_hbm.at[:, cols], w_in.at[k], w_sem.at[0, k])

    def w_out_copy(k):
        rows = pl.ds(pl.multiple_of(tile_of(k) * TILE, TILE), TILE)
        return pltpu.make_async_copy(w_out_hbm.at[rows, :], w_out.at[k], w_sem.at[1, k])

    for k in range(NT):
        w_in_copy(k).start()
    for k in range(NT):
        w_out_copy(k).start()

    def spread(src, dst, n):
        pltpu.make_async_copy(src.at[e], dst.at[0, e], a2a_recv.at[n, 0]).start()

        def far(k, _):
            to = (e + k) % E
            pltpu.make_async_remote_copy(
                src_ref=src.at[to], dst_ref=dst.at[1, e],
                send_sem=a2a_send.at[n, 1], recv_sem=a2a_recv.at[n, 1],
                device_id=(other_dp, to), device_id_type=MESH,
            ).start()
            return 0

        def both(k, _):
            to = (e + k) % E
            pltpu.make_async_remote_copy(
                src_ref=src.at[to], dst_ref=dst.at[0, e],
                send_sem=a2a_send.at[n, 0], recv_sem=a2a_recv.at[n, 0],
                device_id=(d, to), device_id_type=MESH,
            ).start()
            return far(k, 0)

        far(0, 0)
        lax.fori_loop(1, E, both, 0)

    def has_left(src, n):
        wait_bytes(src.at[pl.ds(0, E - 1)], a2a_send.at[n, 0])
        wait_bytes(src, a2a_send.at[n, 1])

    def has_come(dst, n):
        wait_bytes(dst.at[0], a2a_recv.at[n, 0])
        wait_bytes(dst.at[1], a2a_recv.at[n, 1])

    def wait_bytes(ref, sem):
        pltpu.make_async_copy(ref, ref, sem).wait()

    def back(src, dst, n):
        pltpu.make_async_copy(src.at[e], dst.at[e], a2a_recv.at[n, 0]).start()

        def near(k, _):
            to = (e + k) % E
            pltpu.make_async_remote_copy(
                src_ref=src.at[to], dst_ref=dst.at[e],
                send_sem=a2a_send.at[n, 0], recv_sem=a2a_recv.at[n, 0],
                device_id=(d, to), device_id_type=MESH,
            ).start()
            return 0

        lax.fori_loop(1, E, near, 0)

    def pack(parts):
        parts = [p.reshape(E, SPE, D) for p in parts]
        return jnp.concatenate(parts, axis=1).astype(BF)

    parts = []
    logits = []
    inputs[0].wait()
    inputs[1].wait()
    for i in range(PER):
        lg = dot(images[i], router[...], 1, 0)
        logits.append(lg)
        ex = jnp.exp(lg - jnp.max(lg, axis=0, keepdims=True))
        p = ex / jnp.sum(ex, axis=0, keepdims=True)
        disp[i] = p
        parts.append(dot(p.astype(BF), images[i], 0, 0))
    sb_in[...] = pack(parts)
    pl.semaphore_wait(barrier, 2 * E - 1 + 2 * (NZ - 1))
    spread(sb_in, x_rows, 0)
    inputs[2].wait()
    parts = []
    for i in range(PER):
        lg = logits[i]
        ex = jnp.exp(lg - jnp.max(lg, axis=1, keepdims=True))
        p = ex / jnp.sum(ex, axis=1, keepdims=True)
        comb[i] = p
        parts.append(dot(p.astype(BF), out_grad[i], 0, 0))
    packed = pack(parts)
    for p in range(GP):
        sb_grad[p] = packed[:, :, p * GW: (p + 1) * GW]
    spread(sb_grad.at[0], g_rows.at[0], 1)
    has_left(sb_in, 0)
    has_left(sb_grad.at[0], 1)
    spread(sb_grad.at[1], g_rows.at[1], 2)
    spread(sb_grad.at[2], g_rows.at[2], 3)

    def xs():
        return x_rows[...].reshape(2 * ROWS, D)

    def forward(k, _):
        w_in_copy(k).wait()
        pre = dot(xs(), w_in[k], 1, 0)
        sq = pre * pre
        t = jnp.tanh(pre * (C0 + (C0 * C1) * sq))
        half = 0.5 * pre
        hid[k] = (half + half * t).astype(BF)
        gp[k] = (0.5 + 0.5 * t) + half * ((1.0 - t * t) * (C0 + (3.0 * C0 * C1) * sq))
        return 0

    def grad_out(k, p):
        g = dot(hid_t[k], g_rows[p].reshape(2 * ROWS, GW), 1, 0).astype(BF)
        gw_out[p, pl.ds(((1 - z // 4 + k) % 2) * (NZ // 2), NZ // 2)] = g.reshape(NZ // 2, CH_OUT, GW)

    def backward(k, part):
        rows = pl.ds(part * ROWS, ROWS)
        rows_g = jnp.concatenate([g_rows[p, part].reshape(ROWS, GW) for p in range(GP)], axis=1)
        dh = dot(rows_g, w_out[k], 1, 1)
        da[k, rows] = (dh * gp[k, rows]).astype(BF)

    def backward_own(k, _):
        backward(k, 0)
        return 0

    def grad_in(k, _):
        backward(k, 1)
        g = dot(xt[...], da[k], 1, 0)
        gw_in[:, tile_of(k)] = g.reshape(NZ, CH_IN, TILE).astype(BF)
        return 0

    def piece(which, part, c, way=None):
        if which == 0:
            return (part, c) if way is None else (part, c, pl.ds(way * (CH_OUT // 2), CH_OUT // 2))
        first = HALF_T * ((pair + part) % 2)
        return (c, pl.ds(first, HALF_T)) if way is None else (c, pl.ds(first + way, 1))

    def rs_copy(which, part, way, step):
        c = (z + 5 - step) % NZ if way == 0 else (z + 3 + step) % NZ
        mine, half, full = ((gw_out, ro_half, ro_full), (gw_in, ri_half, ri_full))[which]
        src = mine.at[piece(which, part, c, way if step == 1 else None)]
        dst = half.at[part, way] if step == 1 else full.at[part, way, step - 2]
        return pltpu.make_async_remote_copy(
            src_ref=src, dst_ref=dst,
            send_sem=rs_send.at[GP * which + part, way, step - 1], recv_sem=rs_recv.at[GP * which + part, way, step - 1],
            device_id=zdev(1 if way == 0 else NZ - 1), device_id_type=MESH,
        )

    sent = []

    def rs_send_on(which, part, way, step):
        n = len(sent) // 2 - IN_FLIGHT
        if n >= 0:
            rs_copy(*sent[2 * n + way]).wait_send()
        rs_copy(which, part, way, step).start()
        sent.append((which, part, way, step))

    def rs_start(which, part):
        for way in range(2):
            rs_send_on(which, part, way, 1)

    def rs_next(which, part, step):
        mine, half, full = ((gw_out, ro_half, ro_full), (gw_in, ri_half, ri_full))[which]
        for way in range(2):
            rs_copy(which, part, way, step).wait_recv()
            c = (z + 4 - step) % NZ if way == 0 else (z + 4 + step) % NZ
            here = piece(which, part, c, way if step == 1 else None)
            got = half[part, way] if step == 1 else full[part, way, step - 2]
            mine[here] = (mine[here].astype(F32) + got.astype(F32)).astype(BF)
            rs_send_on(which, part, way, step + 1)

    def rs_end(which, part):
        for way in range(2):
            rs_copy(which, part, way, 4).wait_recv()
        if which == 0:
            got = ro_full[part, 0, 2].astype(F32) + ro_full[part, 1, 2].astype(F32)
            w_out_share[:, part * GW: (part + 1) * GW] = (gw_out[part, z].astype(F32) + got).astype(BF)
        else:
            for n in range(HALF_T):
                t = HALF_T * ((pair + part) % 2) + n
                got = ri_full[part, 0, 2, n].astype(F32) + ri_full[part, 1, 2, n].astype(F32)
                cols = pl.ds(pl.multiple_of(t * TILE, TILE), TILE)
                w_in_share[:, cols] = (gw_in[z, t].astype(F32) + got).astype(BF)

    has_come(x_rows, 0)
    lax.fori_loop(0, HALF_T, forward, 0)
    for k in range(HALF_T):
        hid_t[k] = jnp.transpose(hid[k])
    has_come(g_rows.at[0], 1)
    grad_out(0, 0)
    rs_start(0, 0)
    grad_out(1, 0)
    lax.fori_loop(HALF_T, NT, forward, 0)
    off = pl.ds(pl.multiple_of(pair * (D // 2), 128), D // 2)
    xt[...] = jnp.transpose(x_rows[:, :, :, off].reshape(2 * ROWS, D // 2))
    acc = None
    for k in range(NT):
        w_out_copy(k).wait()
        part = dot(hid[k, :ROWS], w_out[k], 1, 0)
        acc = part if acc is None else acc + part
    so_send[...] = acc.astype(BF).reshape(E, BLK, D)
    rs_next(0, 0, 1)
    has_come(g_rows.at[1], 2)
    has_come(g_rows.at[2], 3)
    for p in (1, 2):
        grad_out(0, p)
        rs_start(0, p)
    back(so_send, so_home, 4)
    for p in (1, 2):
        grad_out(1, p)
    lax.fori_loop(0, NT, backward_own, 0)
    rs_next(0, 1, 1)
    acc = dot(da[0, :ROWS], w_in[0], 1, 1)
    for k in range(1, NT):
        acc = acc + dot(da[k, :ROWS], w_in[k], 1, 1)
    dx_send[...] = acc.astype(BF).reshape(E, BLK, D)
    back(dx_send, dx_home, 5)
    rs_next(0, 2, 1)
    lax.fori_loop(0, HALF_T, grad_in, 0)
    rs_start(1, 0)
    rs_next(0, 0, 2)
    lax.fori_loop(HALF_T, NT, grad_in, 0)
    rs_start(1, 1)
    rs_next(0, 1, 2)
    rs_next(0, 2, 2)

    def home(ref, i):
        return ref[...].astype(F32).reshape(E, PER, SPE, D)[:, i].reshape(S, D).astype(BF)

    wait_bytes(so_home, a2a_recv.at[4, 0])
    first = []
    for i in range(PER):
        dc = dot(out_grad[i], home(so_home, i), 1, 1)
        cm = comb[i]
        first.append(cm * (dc - jnp.sum(cm * dc, axis=1, keepdims=True)))
    wait_bytes(dx_home, a2a_recv.at[5, 0])
    rs_next(1, 0, 1)
    total = jnp.zeros((S, D), F32)
    for i in range(PER):
        dx = home(dx_home, i)
        dd = dot(images[i], dx, 1, 1)
        dm = disp[i]
        dl = (first[i] + dm * (dd - jnp.sum(dm * dd, axis=0, keepdims=True))).astype(BF)
        total = total + dot(dl, images[i], 0, 0)
        image_grad[i] = (dot(dm.astype(BF), dx, 1, 0) + dot(dl, router[...], 1, 1)).astype(BF)
    total = total.reshape(E, SPE, D)
    rpart[...] = jnp.concatenate([total[:, :, : D // 2], total[:, :, D // 2:]], axis=1).astype(BF)

    pltpu.make_async_copy(rpart.at[e], r_a.at[e], ar_recv.at[0]).start()

    def send_a(k, _):
        to = (e + k) % E
        pltpu.make_async_remote_copy(
            src_ref=rpart.at[to], dst_ref=r_a.at[e], send_sem=ar_send.at[0], recv_sem=ar_recv.at[0],
            device_id=(d, to), device_id_type=MESH,
        ).start()
        return 0

    lax.fori_loop(1, E, send_a, 0)
    rs_next(1, 1, 1)
    rs_next(0, 0, 3)
    wait_bytes(r_a, ar_recv.at[0])
    summed = jnp.sum(r_a[...].astype(F32), axis=0)
    for h in range(2):
        for r in range(SPE):
            b_rows[h * SPE + r] = summed[h * SPE + r: h * SPE + r + 1, :]

    def to_column(src_of, dst, n):
        pltpu.make_async_copy(src_of(pair, z), dst.at[pair, z], ar_recv.at[n]).start()
        for k in range(NZ):
            to = (z + k) % NZ
            if k:
                pltpu.make_async_remote_copy(
                    src_ref=src_of(pair, to), dst_ref=dst.at[pair, z], send_sem=ar_send.at[n], recv_sem=ar_recv.at[n],
                    device_id=zdev(k), device_id_type=MESH,
                ).start()
            pltpu.make_async_remote_copy(
                src_ref=src_of(1 - pair, to), dst_ref=dst.at[pair, z], send_sem=ar_send.at[n], recv_sem=ar_recv.at[n],
                device_id=zdev_other(k), device_id_type=MESH,
            ).start()

    to_column(lambda h, r: b_rows.at[h * NZ + r], r_b2, 1)
    rs_next(1, 0, 2)
    rs_next(0, 1, 3)
    wait_bytes(r_b2, ar_recv.at[1])
    c_row[0] = jnp.sum(r_b2[...].reshape(2 * NZ, 1, D // 2), axis=0)
    to_column(lambda h, r: c_row.at[0], r_b3, 2)
    rs_next(0, 2, 3)
    rs_next(1, 1, 2)
    wait_bytes(r_b3, ar_recv.at[2])
    for h in range(2):
        for r in range(SPE):
            c_mine[r:r + 1, h * (D // 2): (h + 1) * (D // 2)] = r_b3[h, r]
    pltpu.make_async_copy(c_mine, r_c.at[e], ar_recv.at[3]).start()

    def send_c(k, _):
        pltpu.make_async_remote_copy(
            src_ref=c_mine, dst_ref=r_c.at[e], send_sem=ar_send.at[3], recv_sem=ar_recv.at[3],
            device_id=(d, (e + k) % E), device_id_type=MESH,
        ).start()
        return 0

    lax.fori_loop(1, E, send_c, 0)
    rs_next(1, 0, 3)
    rs_next(1, 1, 3)
    for p in range(GP):
        rs_end(0, p)
    wait_bytes(r_c, ar_recv.at[3])
    router_grad[...] = r_c[...]
    rs_end(1, 0)
    rs_end(1, 1)

    has_left(sb_grad.at[1], 2)
    has_left(sb_grad.at[2], 3)
    for n in (4, 5):
        wait_bytes(so_send.at[pl.ds(0, E - 1)], a2a_send.at[n, 0])
    for last in sent[-2 * IN_FLIGHT:]:
        rs_copy(*last).wait_send()
    wait_bytes(rpart.at[pl.ds(0, E - 1)], ar_send.at[0])
    for n in (1, 2):
        wait_bytes(b_rows.at[pl.ds(0, 2 * NZ - 1)], ar_send.at[n])
    wait_bytes(r_c.at[pl.ds(0, E - 1)], ar_send.at[3])


def deliver(image_grad_in, router_grad_in, w_in_in, w_out_in, image_grad, router_grad, w_in_share, w_out_share, router_held, sem):
    copies = [
        pltpu.make_async_copy(image_grad_in, image_grad, sem.at[0]),
        pltpu.make_async_copy(w_in_in, w_in_share.at[0], sem.at[1]),
        pltpu.make_async_copy(w_out_in, w_out_share.at[0], sem.at[2]),
        pltpu.make_async_copy(router_held, router_grad, sem.at[3]),
    ]
    for c in copies[:3]:
        c.start()
    router_held[...] = jnp.transpose(router_grad_in[...].reshape(S, D))
    copies[3].start()
    for c in copies:
        c.wait()


def local(images, out_grad, router, w_in, w_out):
    hbm = pl.BlockSpec(memory_space=pltpu.HBM)
    vm = pl.BlockSpec(memory_space=pltpu.VMEM)
    V = pltpu.VMEM
    DMA = pltpu.SemaphoreType.DMA
    parts = pl.pallas_call(
        kernel,
        out_shape=(V((PER, M, D), BF), V((E, SPE, D), F32), V((CH_IN, H), BF), V((CH_OUT, D), BF)),
        in_specs=[hbm] * 5,
        out_specs=(vm,) * 4,
        scratch_shapes=[
            V((PER, M, D), BF), V((PER, M, D), BF), V((D, S), BF),
            V((NT, D, TILE), BF), V((NT, TILE, D), BF),
            V((PER, M, S), F32), V((PER, M, S), F32),
            V((E, BLK, D), BF), V((GP, E, BLK, GW), BF),
            V((2, E, BLK, D), BF), V((GP, 2, E, BLK, GW), BF),
            V((NT, 2 * ROWS, TILE), BF), V((HALF_T, TILE, 2 * ROWS), BF), V((NT, 2 * ROWS, TILE), F32), V((NT, 2 * ROWS, TILE), BF),
            V((D // 2, 2 * ROWS), BF),
            V((GP, NZ, CH_OUT, GW), BF), V((NZ, NT, CH_IN, TILE), BF),
            V((GP, 2, CH_OUT // 2, GW), BF), V((GP, 2, 3, CH_OUT, GW), BF),
            V((2, 2, 1, CH_IN, TILE), BF), V((2, 2, 3, HALF_T, CH_IN, TILE), BF),
            V((E, BLK, D), BF), V((E, BLK, D), BF), V((E, BLK, D), BF), V((E, BLK, D), BF),
            V((E, 2 * SPE, D // 2), BF), V((E, 2 * SPE, D // 2), BF),
            V((2 * NZ, 1, D // 2), F32), V((2, NZ, 1, D // 2), F32),
            V((1, 1, D // 2), F32), V((2, NZ, 1, D // 2), F32), V((SPE, D), F32), V((E, SPE, D), F32),
            DMA((2, NT)), DMA((3,)),
            DMA((6, 2)), DMA((6, 2)),
            DMA((GP + 2, 2, 4)), DMA((GP + 2, 2, 4)),
            DMA((4,)), DMA((4,)),
        ],
        compiler_params=pltpu.CompilerParams(
            collective_id=0, has_side_effects=True, vmem_limit_bytes=62 * 1024 * 1024
        ),
    )(images, out_grad, router, w_in[0], w_out[0])
    return pl.pallas_call(
        deliver,
        out_shape=(
            jax.ShapeDtypeStruct((PER, M, D), BF),
            jax.ShapeDtypeStruct((D, S), F32),
            jax.ShapeDtypeStruct((1, CH_IN, H), BF),
            jax.ShapeDtypeStruct((1, CH_OUT, D), BF),
        ),
        in_specs=[vm] * 4,
        out_specs=(hbm,) * 4,
        scratch_shapes=[V((D, S), F32), DMA((4,))],
        compiler_params=pltpu.CompilerParams(vmem_limit_bytes=16 * 1024 * 1024),
    )(*parts)


def solution(mesh):
    return jax.shard_map(
        local,
        mesh=mesh,
        in_specs=(
            P(("dp", "expert"), None, None),
            P(("dp", "expert"), None, None),
            P(),
            P("expert", None, None),
            P("expert", None, None),
        ),
        out_specs=(
            P(("dp", "expert"), None, None),
            P(),
            P("expert", "dp", None),
            P("expert", "dp", None),
        ),
        check_vma=False,
    )
```

time: 86.7 us -> 83.7 us (0.965)
  the two profiles are of different devices: /device:TPU:8 before, /device:TPU:1 now
where the time goes in v3:
time: 83.7 us; the launch traced here: 82.7 us
  Pallas kernels  82.1 us (98%)
    pallas_call x1, Pallas kernels, local(): pl.pallas_call(kernel, out_shape=(V((PER, M, D), BF), V((E, SPE, D), F32)...  80.8 us

profile of v3, /device:TPU:1, one launch (start us, length us, event | category | flops | bytes accessed | tf_op | source)
XLA Modules:
  0.0 82.7 jit_solution(417687351608816690)
XLA Ops:
  0.6 80.8 %shard_map.84 = (bf16[2,256,768]{2,1,0:T(8,128)(2,1)S(1)}, f32[16,8,768]{2,1,0:T(8,128)S(1)}, bf16[48,3072]{1,0:T(8,128)(2,1)S(1)}, bf16[192,768]{1,0:T(8,128)(2,1)S(1)}) custom-call(bf16[2,256,768]{2,1,0:T(8,128)(2,1)} %images_hbm.1, bf16[2,256,768]{2,1,0:T(8,128)(2,1)} %out_grad_hbm.1, bf16[768,128]{1,0:T(8,128)(2,1)} %router_hbm.1, ...), custom_call_target="tpu_custom_call" | custom-call | tf_op jit(solution)/shard_map/pallas_call | solution.py:433
  81.5 1.2 %shard_map.85 = (bf16[2,256,768]{2,1,0:T(8,128)(2,1)}, f32[768,128]{1,0:T(8,128)}, bf16[1,48,3072]{2,1,0:T(8,128)(2,1)}, bf16[1,192,768]{2,1,0:T(8,128)(2,1)}) custom-call(bf16[2,256,768]{2,1,0:T(8,128)(2,1)S(1)} %get-tuple-element.8.image_grad_in, f32[16,8,768]{2,1,0:T(8,128)S(1)} %get-tuple-element.9.router_grad_in, ...), custom_call_target="tpu_custom_call" | custom-call | tf_op jit(solution)/shard_map/pallas_call | solution.py:462

commit v4 on v3

--- a/solution.py
+++ b/solution.py
@@ -60,22 +60,6 @@
     def zdev_other(k):
         return ((1 - pair) * NZ + (z + k) % NZ, e)
 
-    barrier = pltpu.get_barrier_semaphore()
-
-    def greet(k, _):
-        pl.semaphore_signal(barrier, inc=1, device_id=(other_dp, (e + k) % E), device_id_type=MESH)
-        return 0
-
-    def greet_own(k, _):
-        pl.semaphore_signal(barrier, inc=1, device_id=(d, (e + k) % E), device_id_type=MESH)
-        return 0
-
-    lax.fori_loop(0, E, greet, 0)
-    lax.fori_loop(1, E, greet_own, 0)
-    for k in range(1, NZ):
-        pl.semaphore_signal(barrier, inc=1, device_id=zdev(k), device_id_type=MESH)
-        pl.semaphore_signal(barrier, inc=1, device_id=zdev_other(k), device_id_type=MESH)
-
     inputs = [
         pltpu.make_async_copy(images_hbm, images, io_sem.at[0]),
         pltpu.make_async_copy(router_hbm, router, io_sem.at[1]),
@@ -84,6 +68,22 @@
     for c in inputs:
         c.start()
 
+    barrier = pltpu.get_barrier_semaphore()
+
+    def greet(k, _):
+        pl.semaphore_signal(barrier, inc=1, device_id=(other_dp, (e + k) % E), device_id_type=MESH)
+        return 0
+
+    def greet_own(k, _):
+        pl.semaphore_signal(barrier, inc=1, device_id=(d, (e + k) % E), device_id_type=MESH)
+        return 0
+
+    lax.fori_loop(0, E, greet, 0)
+    lax.fori_loop(1, E, greet_own, 0)
+    for k in range(1, NZ):
+        pl.semaphore_signal(barrier, inc=1, device_id=zdev(k), device_id_type=MESH)
+        pl.semaphore_signal(barrier, inc=1, device_id=zdev_other(k), device_id_type=MESH)
+
     def tile_of(k):
         return 2 * ((pair + k // 2) % 2) + (1 - z // 4 + k) % 2
 
@@ -94,11 +94,6 @@
     def w_out_copy(k):
         rows = pl.ds(pl.multiple_of(tile_of(k) * TILE, TILE), TILE)
         return pltpu.make_async_copy(w_out_hbm.at[rows, :], w_out.at[k], w_sem.at[1, k])
-
-    for k in range(NT):
-        w_in_copy(k).start()
-    for k in range(NT):
-        w_out_copy(k).start()
 
     def spread(src, dst, n):
         pltpu.make_async_copy(src.at[e], dst.at[0, e], a2a_recv.at[n, 0]).start()
@@ -155,8 +150,13 @@
 
     parts = []
     logits = []
+    inputs[1].wait()
     inputs[0].wait()
-    inputs[1].wait()
+    inputs[2].wait()
+    for k in range(NT):
+        w_in_copy(k).start()
+    for k in range(NT):
+        w_out_copy(k).start()
     for i in range(PER):
         lg = dot(images[i], router[...], 1, 0)
         logits.append(lg)
@@ -167,7 +167,6 @@
     sb_in[...] = pack(parts)
     pl.semaphore_wait(barrier, 2 * E - 1 + 2 * (NZ - 1))
     spread(sb_in, x_rows, 0)
-    inputs[2].wait()
     parts = []
     for i in range(PER):
         lg = logits[i]

time: 83.7 us -> 82.8 us (0.989); the launches traced: 82.7 us -> 82.7 us
  no operation moved by 1% of the time
where the time goes in v4:
time: 82.8 us; the launch traced here: 82.7 us
  Pallas kernels  82.1 us (99%)
    pallas_call x1, Pallas kernels, local(): pl.pallas_call(kernel, out_shape=(V((PER, M, D), BF), V((E, SPE, D), F32)...  80.8 us

profile of v4, /device:TPU:1, one launch (start us, length us, event | category | flops | bytes accessed | tf_op | source)
XLA Modules:
  0.0 82.7 jit_solution(2836315980404552915)
XLA Ops:
  0.6 80.8 %shard_map.84 = (bf16[2,256,768]{2,1,0:T(8,128)(2,1)S(1)}, f32[16,8,768]{2,1,0:T(8,128)S(1)}, bf16[48,3072]{1,0:T(8,128)(2,1)S(1)}, bf16[192,768]{1,0:T(8,128)(2,1)S(1)}) custom-call(bf16[2,256,768]{2,1,0:T(8,128)(2,1)} %images_hbm.1, bf16[2,256,768]{2,1,0:T(8,128)(2,1)} %out_grad_hbm.1, bf16[768,128]{1,0:T(8,128)(2,1)} %router_hbm.1, ...), custom_call_target="tpu_custom_call" | custom-call | tf_op jit(solution)/shard_map/pallas_call | solution.py:432
  81.5 1.2 %shard_map.85 = (bf16[2,256,768]{2,1,0:T(8,128)(2,1)}, f32[768,128]{1,0:T(8,128)}, bf16[1,48,3072]{2,1,0:T(8,128)(2,1)}, bf16[1,192,768]{2,1,0:T(8,128)(2,1)}) custom-call(bf16[2,256,768]{2,1,0:T(8,128)(2,1)S(1)} %get-tuple-element.8.image_grad_in, f32[16,8,768]{2,1,0:T(8,128)S(1)} %get-tuple-element.9.router_grad_in, ...), custom_call_target="tpu_custom_call" | custom-call | tf_op jit(solution)/shard_map/pallas_call | solution.py:461
